TPU v7x, 32 devices: a whole 2x2x4 slice. The times are simulated.
32 devices in a mesh: section: 4 (over x, core), tensor: 8 (over z, y).
Axes of the slice: x: 2, y: 2, z: 4, core: 2. Of those that a mesh axis runs over, the one named last changes fastest.
Arguments:
- hidden: bfloat16 [2048, 14336], P('section', 'tensor'), may hold values from -6 to 6
- down_weight: bfloat16 [4, 14336, 4096], P('section', 'tensor'), may hold values from -0.046875 to 0.046875
- down_shrink: bfloat16 [4, 14336, 256], P('section', 'tensor'), may hold values from -0.046875 to 0.046875
- down_up_factors: bfloat16 [4, 256, 4096], P('section', None, 'tensor'), may hold values from -0.5 to 0.5
- residual: bfloat16 [2048, 4096], P(('section', 'tensor')), may hold values from -6 to 6
- tenant_ids: int32 [2048], P('section'), may hold values from 0 to 3
- adapter_rank: int32 [4], replicated, may hold values from 16 to 128, as said below
- adapter_offset: int32 [4], replicated, may hold values from 0 to 224, as said below
- norm_gain: bfloat16 [4, 4096], P('section'), may hold values from 0.099609375 to 1.8984375
- qkv_weight: bfloat16 [4, 4096, 5120], P('section', None, 'tensor'), may hold values from -0.09375 to 0.09375
- qkv_shrink: bfloat16 [4, 4096, 256], P('section', None, 'tensor'), may hold values from -0.09375 to 0.09375
- qkv_expand: bfloat16 [4, 256, 5120], P('section', None, 'tensor'), may hold values from -0.5 to 0.5
Outputs:
- stream: bfloat16 [2048, 4096], P(('section', 'tensor'))
- qkv: bfloat16 [2048, 5120], P('section', 'tensor')
Inputs may be any that keep to these rules, and one draw needn't show every extreme that they name: `adapter_rank`: every rank is a multiple of 16; one tenant has rank 256 // 2, the last tenant has rank 256 // 16; the ranks sum to exactly 240. `adapter_offset`: the exclusive prefix sums of adapter_rank in tenant order.
All inputs are finite; a program needn't handle non-finite values.
Results may differ from a plain program's by a relative error of at most 0.02.
Values may be sent and summed in bfloat16 or wider, within the bound.
A program may use at most 64 MiB of HBM per device.

v0:
```python
import jax
import jax.numpy as jnp
from jax import lax
from jax.sharding import PartitionSpec as P

adapter_alpha_scale = 32.0


def passed_along(block, axis, distance):
    devices = range(lax.axis_size(axis))
    route = [((i - distance) % len(devices), i) for i in devices]
    return lax.ppermute(block, axis, route)


def table_lookup(table, tenants):
    chosen = tenants[:, None] == jnp.arange(table.shape[0], dtype=jnp.int32)[None, :]
    return jnp.sum(jnp.where(chosen, table[None, :], 0), axis=1)


def adapter_scale(tenants, adapter_rank, adapter_offset, first_col, col_count):
    lower = table_lookup(adapter_offset, tenants)
    tenant_ranks = table_lookup(adapter_rank, tenants)
    columns = first_col + jnp.arange(col_count, dtype=jnp.int32)
    inside = (columns[None, :] >= lower[:, None]) & (
        columns[None, :] < (lower + tenant_ranks)[:, None]
    )
    scaling_factor = adapter_alpha_scale / tenant_ranks.astype(jnp.float32)
    return jnp.where(inside, scaling_factor[:, None], jnp.float32(0.0))


def rounded(values):
    return lax.optimization_barrier(values.astype(jnp.bfloat16)).astype(jnp.float32)


def per_device(
    hidden,
    down_weight,
    down_shrink,
    down_up_factors,
    residual,
    tenant_ids,
    adapter_rank,
    adapter_offset,
    norm_gain,
    qkv_weight,
    qkv_shrink,
    qkv_expand,
):
    down_matrix = down_weight[0]
    down_factor = down_shrink[0]
    group_size = lax.axis_size("tensor")
    my_index = lax.axis_index("tensor")
    row_count = hidden.shape[0]
    share_rows = row_count // group_size
    rank_total = down_factor.shape[1]
    my_tenants = lax.dynamic_slice_in_dim(tenant_ids, my_index * share_rows, share_rows, 0)
    expand_full = lax.all_gather(down_up_factors[0], "tensor", axis=1, tiled=True)
    shrunk = lax.psum(
        rounded(jnp.dot(hidden, down_factor, preferred_element_type=jnp.float32)).astype(
            jnp.bfloat16
        ),
        "tensor",
    ).astype(jnp.float32)
    my_shrunk = lax.dynamic_slice_in_dim(shrunk, my_index * share_rows, share_rows, 0)
    base = lax.psum_scatter(
        rounded(jnp.dot(hidden, down_matrix, preferred_element_type=jnp.float32)).astype(
            jnp.bfloat16
        ),
        "tensor",
        scatter_dimension=0,
        tiled=True,
    ).astype(jnp.float32)
    small_rows = (
        my_shrunk * adapter_scale(my_tenants, adapter_rank, adapter_offset, 0, rank_total)
    ).astype(jnp.bfloat16)
    down_out = base + jnp.dot(small_rows, expand_full, preferred_element_type=jnp.float32)
    stream = (residual.astype(jnp.float32) + down_out).astype(jnp.bfloat16)
    arrived, id_codes = passed_along((stream, tenant_ids.astype(jnp.bfloat16)), "section", 1)
    arrived_ids = id_codes.astype(jnp.int32)
    values = arrived.astype(jnp.float32)
    inverse = lax.rsqrt(jnp.mean(values * values, axis=-1, keepdims=True) + 1e-05)
    normed = (values * inverse * norm_gain[0].astype(jnp.float32)[None, :]).astype(jnp.bfloat16)
    complete_rows = lax.all_gather(normed, "tensor", axis=0, tiled=True)
    rank_cols = qkv_shrink.shape[2]
    shrunk_part = jnp.dot(complete_rows, qkv_shrink[0], preferred_element_type=jnp.float32)
    scaled_part = (
        shrunk_part
        * adapter_scale(arrived_ids, adapter_rank, adapter_offset, my_index * rank_cols, rank_cols)
    ).astype(jnp.bfloat16)
    small_all = lax.all_gather(scaled_part, "tensor", axis=1, tiled=True)
    query_key_value_output = jnp.dot(
        complete_rows, qkv_weight[0], preferred_element_type=jnp.float32
    ) + jnp.dot(small_all, qkv_expand[0], preferred_element_type=jnp.float32)
    return (stream, query_key_value_output.astype(jnp.bfloat16))


def solution(mesh):
    in_specs = (
        P("section", "tensor"),
        P("section", "tensor", None),
        P("section", "tensor", None),
        P("section", None, "tensor"),
        P(("section", "tensor"), None),
        P("section"),
        P(),
        P(),
        P("section", None),
        P("section", None, "tensor"),
        P("section", None, "tensor"),
        P("section", None, "tensor"),
    )
    out_specs = (P(("section", "tensor"), None), P("section", "tensor"))
    return jax.shard_map(
        per_device, mesh=mesh, in_specs=in_specs, out_specs=out_specs, check_vma=False
    )
```

profile of v0, /device:TPU:0, one launch (start us, length us, event | category | flops | bytes accessed | tf_op | source)
XLA Modules:
  0.0 361.9 jit_solution(2810671696461541055)
XLA Ops:
  7.2 0.0 copy-start
  7.2 0.0 all-reduce.2.cloned.1.call-start
  7.2 1.4 copy-done
  8.7 2.5 convolution_convert_fusion
  11.2 0.0 all-reduce.2.cloned.1.call-update
  11.2 0.0 all-gather.6.cloned.1.call-start
  11.3 0.7 all-gather.6.cloned.1.call-update
  12.0 0.0 reduce-scatter.2.cloned.1.call-start
  12.0 12.4 %fusion.2 = bf16[512,4096]{1,0:T(8,128)(2,1)} fusion(bf16[512,1792]{1,0:T(8,128)(2,1)S(1)} %copy-done, bf16[1,1792,4096]{2,1,0:T(8,128)(2,1)} %param.13), kind=kOutput, calls=%fused_computation.2 | convolution fusion | flops 7518289920 | bytes 20709376 | tf_op jit(solution)/shard_map/dot_general | solution.py:66
  24.4 0.0 copy-start.9
  24.4 0.0 copy-start.7
  24.4 0.0 copy-start.8
  24.4 0.0 copy-start.2
  24.4 0.0 copy-start.6
  24.4 0.0 copy-start.5
  24.4 0.0 reduce-scatter.2.cloned.1.call-update
  24.5 0.0 all-gather.4.cloned.1.call-start
  24.5 0.6 copy-done.9
  25.1 0.1 dynamic_slice.7
  25.1 0.0 copy-done.7
  25.2 0.0 copy-done.8
  25.2 0.1 select_reduce_fusion.3
  25.3 59.9 %all-reduce.2.cloned.1.call-done = bf16[512,256]{1,0:T(8,128)(2,1)} async-done(((bf16[512,256]{1,0:T(8,128)(2,1)}), bf16[512,256]{1,0:T(8,128)(2,1)}) %all-reduce.2.cloned.1.call-update) | async-done | bytes 262160 | tf_op jit(solution)/shard_map/psum | solution.py:58
  85.2 52.6 %all-gather.6.cloned.1.call-done = bf16[1,256,4096]{2,1,0:T(8,128)(2,1)} async-done(((bf16[1,256,512]{2,1,0:T(8,128)(2,1)}), bf16[1,256,4096]{2,1,0:T(8,128)(2,1)}) %all-gather.6.cloned.1.call-update) | async-done | bytes 2097168 | tf_op jit(solution)/shard_map/all_gather | solution.py:57
  137.8 90.4 %reduce-scatter.2.cloned.1.call-done = bf16[64,4096]{1,0:T(8,128)(2,1)} async-done(((bf16[512,4096]{1,0:T(8,128)(2,1)}), bf16[64,4096]{1,0:T(8,128)(2,1)}) %reduce-scatter.2.cloned.1.call-update) | async-done | bytes 524304 | tf_op jit(solution)/shard_map/reduce_scatter | solution.py:65
  228.2 0.0 copy-done.2
  228.2 2.3 fusion.8
  230.4 0.0 copy-start.3
  230.4 0.1 collective-permute-start
  230.5 0.0 copy-done.6
  230.5 8.6 %collective-permute-done = bf16[64,4096]{1,0:T(8,128)(2,1)S(1)} collective-permute-done((bf16[64,4096]{1,0:T(8,128)(2,1)S(1)}, bf16[64,4096]{1,0:T(8,128)(2,1)S(1)}, u32[]{:S(2)}, u32[]{:S(2)}) %collective-permute-start) | collective-permute-done | bytes 524320 | tf_op jit(solution)/shard_map/ppermute | solution.py:12
  239.1 0.2 fusion.12
  239.3 1.0 fusion.14
  240.3 0.0 all-gather.4.cloned.1.call-update
  240.3 0.1 collective-permute-start.1
  240.4 3.0 collective-permute-done.1
  243.4 0.1 select_reduce_fusion.1
  243.5 70.1 %all-gather.4.cloned.1.call-done = bf16[512,4096]{1,0:T(8,128)(2,1)} async-done(((bf16[64,4096]{1,0:T(8,128)(2,1)}), bf16[512,4096]{1,0:T(8,128)(2,1)}) %all-gather.4.cloned.1.call-update) | async-done | bytes 4194320 | tf_op jit(solution)/shard_map/all_gather | solution.py:83
  313.6 0.0 copy-done.5
  313.6 0.0 copy-start.1
  313.6 3.7 %fusion.11 = bf16[512,32]{0,1:T(8,128)(2,1)S(1)} fusion(bf16[512,4096]{1,0:T(8,128)(2,1)} %all-gather.4.cloned.1.call-done, bf16[1,4096,32]{1,2,0:T(8,128)(2,1)S(1)} %copy-done.5, f32[512]{0:T(512)S(1)} %convert_divide_fusion, s32[512]{0:T(512)S(1)} %add.60, s32[512]{0:T(512)S(1)} %get-tuple-element.2, s32[32]{0:T(128)S(1)} %iota_add_fusion), kind=kOutput, calls=%fused_computation.15 | convolution fusion | flops 134316032 | bytes 4495488 | tf_op jit(solution)/shard_map/dot_general | solution.py:85
  317.3 30.7 %all_gather.11 = bf16[512,256]{0,1:T(8,128)(2,1)S(1)} all-gather(bf16[512,32]{0,1:T(8,128)(2,1)S(1)} %fusion.11), channel_id=1, replica_groups=mesh['section'=4,'tensor'=8] {'tensor'}, dimensions={1}, use_global_device_ids=true | all-gather | bytes 294912 | tf_op jit(solution)/shard_map/all_gather | solution.py:90
  348.1 0.0 copy-done.1
  348.1 0.0 copy-start.4
  348.1 6.0 %fusion.5 = f32[512,640]{1,0:T(8,128)S(1)} fusion(bf16[512,4096]{1,0:T(8,128)(2,1)S(1)} %copy-done.1, bf16[1,4096,640]{2,1,0:T(8,128)(2,1)} %param.21), kind=kOutput, calls=%fused_computation.3 | convolution fusion | flops 2684354560 | bytes 10747904 | tf_op jit(solution)/shard_map/dot_general | solution.py:91
  354.1 0.0 copy-done.3
  354.1 0.0 copy-done.4
  354.1 1.2 fusion.10
  (9 shorter events, 0.1 us)
Async XLA Ops:
  7.2 1.5 copy-start
  7.2 78.0 %all-reduce.2.cloned.1.call-start = ((), (), s32[]{:S(2)}) async-start(), calls=%async_computation.2 | async-start | bytes 524288 | tf_op jit(solution)/shard_map/psum | solution.py:58
  11.2 126.6 %all-gather.6.cloned.1.call-start = ((), (), s32[]{:S(2)}) async-start(), calls=%async_computation.4 | async-start | bytes 2359296 | tf_op jit(solution)/shard_map/all_gather | solution.py:57
  12.0 216.2 %reduce-scatter.2.cloned.1.call-start = ((), (), s32[]{:S(2)}) async-start(), calls=%async_computation.1 | async-start | bytes 4718592 | tf_op jit(solution)/shard_map/reduce_scatter | solution.py:65
  24.4 0.7 copy-start.9
  24.4 0.8 copy-start.7
  24.4 0.8 copy-start.8
  24.4 203.8 %copy-start.2 = (bf16[64,4096]{1,0:T(8,128)(2,1)S(1)}, bf16[64,4096]{1,0:T(8,128)(2,1)}, u32[]{:S(2)}) copy-start(bf16[64,4096]{1,0:T(8,128)(2,1)} %param.16) | copy-start | bytes 1572868
  24.4 206.1 %copy-start.6 = (bf16[1,4096]{1,0:T(2,128)(2,1)S(1)}, bf16[1,4096]{1,0:T(2,128)(2,1)}, u32[]{:S(2)}) copy-start(bf16[1,4096]{1,0:T(2,128)(2,1)} %param.20) | copy-start | bytes 24580
  24.4 289.2 %copy-start.5 = (bf16[1,4096,32]{1,2,0:T(8,128)(2,1)S(1)}, bf16[1,4096,32]{1,2,0:T(8,128)(2,1)}, u32[]{:S(2)}) copy-start(bf16[1,4096,32]{1,2,0:T(8,128)(2,1)} %param.22) | copy-start | bytes 786436
  24.5 289.2 %all-gather.4.cloned.1.call-start = ((), (), s32[]{:S(2)}) async-start(), calls=%async_computation.3 | async-start | bytes 4718592 | tf_op jit(solution)/shard_map/all_gather | solution.py:83
  230.4 123.6 %copy-start.3 = (bf16[64,4096]{1,0:T(8,128)(2,1)}, bf16[64,4096]{1,0:T(8,128)(2,1)S(1)}, u32[]{:S(2)}) copy-start(bf16[64,4096]{1,0:T(8,128)(2,1)S(1)} %fusion.8) | copy-start | bytes 1572868
  230.4 8.7 %collective-permute-start = (bf16[64,4096]{1,0:T(8,128)(2,1)S(1)}, bf16[64,4096]{1,0:T(8,128)(2,1)S(1)}, u32[]{:S(2)}, u32[]{:S(2)}) collective-permute-start(bf16[64,4096]{1,0:T(8,128)(2,1)S(1)} %fusion.8), channel_id=1, source_target_pairs={{24,0},{0,8},{8,16},{16,24},{25,1},{1,9},{9,17},{17,25},{26,2},{2,... | collective-permute-start | bytes 1572872 | tf_op jit(solution)/shard_map/ppermute | solution.py:12
  240.3 3.0 collective-permute-start.1
  313.6 34.4 %copy-start.1 = (bf16[512,4096]{1,0:T(8,128)(2,1)S(1)}, bf16[512,4096]{1,0:T(8,128)(2,1)}, u32[]{:S(2)}) copy-start(bf16[512,4096]{1,0:T(8,128)(2,1)} %all-gather.4.cloned.1.call-done) | copy-start | bytes 12582916
  348.1 6.0 %copy-start.4 = (bf16[1,256,640]{2,1,0:T(8,128)(2,1)S(1)}, bf16[1,256,640]{2,1,0:T(8,128)(2,1)}, u32[]{:S(2)}) copy-start(bf16[1,256,640]{2,1,0:T(8,128)(2,1)} %param.23) | copy-start | bytes 983044
Sparse Core Ops, SparseCore 0:
  11.9 73.2 all-reduce.1
  87.4 50.3 all-gather.5
  141.9 86.2 reduce-scatter.1
  240.4 73.1 all-gather.3
where the time goes:
time: 362 us
  waiting for transfers between devices  285 us (79%)
  blocking collectives  30.7 us (8%)
  matrix products  28.1 us (8%)
  between operations  13.9 us (4%)
    reduce_scatter x1, waiting for transfers between devices, per_device(): lax.psum_scatter(rounded(jnp.dot(hidden, down_matrix, preferred_element_t...  90.4 us
    all_gather x1, waiting for transfers between devices, per_device(): complete_rows = lax.all_gather(normed, 'tensor', axis=0, tiled=True)  70.1 us
    psum x1, waiting for transfers between devices, per_device(): lax.psum(rounded(jnp.dot(hidden, down_factor, preferred_element_type=jnp....  59.9 us
    all_gather x1, waiting for transfers between devices, per_device(): lax.all_gather(down_up_factors[0], 'tensor', axis=1, tiled=True)  52.6 us
    all_gather x1, blocking collectives, per_device(): small_all = lax.all_gather(scaled_part, 'tensor', axis=1, tiled=True)  30.7 us
    dot_general x1, matrix products, per_device(): jnp.dot(hidden, down_matrix, preferred_element_type=jnp.float32)  12.4 us
    ppermute x2, waiting for transfers between devices, passed_along(): return lax.ppermute(block, axis, route)  11.5 us
  transfers between devices with their start and end apart: 6, of which 6 were waited for; matrix products, arithmetic and copies ran while one was open for 4% of the time, Pallas kernels for 0%

commit v1 on v0

v1 whole, which is shorter than its diff:
```python
import functools

import jax
import jax.numpy as jnp
from jax import lax
from jax.experimental import pallas as pl
from jax.experimental.pallas import tpu as pltpu
from jax.sharding import PartitionSpec as P

adapter_alpha_scale = 32.0
MESH = pl.DeviceIdType.MESH
F32 = jnp.float32
BF16 = jnp.bfloat16
CHUNK = 16
WIDE = 512


def table_lookup(table, tenants):
    chosen = tenants[:, None] == jnp.arange(table.shape[0], dtype=jnp.int32)[None, :]
    return jnp.sum(jnp.where(chosen, table[None, :], 0), axis=1)


def adapter_scale(tenants, adapter_rank, adapter_offset, first_col, col_count):
    lower = table_lookup(adapter_offset, tenants)
    tenant_ranks = table_lookup(adapter_rank, tenants)
    columns = first_col + jnp.arange(col_count, dtype=jnp.int32)
    inside = (columns[None, :] >= lower[:, None]) & (
        columns[None, :] < (lower + tenant_ranks)[:, None]
    )
    scaling_factor = adapter_alpha_scale / tenant_ranks.astype(jnp.float32)
    return jnp.where(inside, scaling_factor[:, None], jnp.float32(0.0))


def kernel(
    T,
    S,
    hidden_in,
    down_in,
    shrink_in,
    up_in,
    residual_in,
    gain_ref,
    qkv_in,
    qshrink_in,
    expand_in,
    scale_ref,
    scale_t_in,
    stream_ref,
    out_ref,
    hidden,
    down,
    shrink,
    up,
    residual,
    qkv_w,
    qshrink,
    expand,
    partial,
    lhs,
    low_mine,
    low_in,
    dlow,
    ex_out,
    ex_in,
    rs,
    arrived,
    scale_t,
    ag,
    lhs2,
    acc,
    qlow,
    qlow_all,
    load_sem,
    down_sem,
    low_ss,
    low_rs,
    dlow_ss,
    dlow_rs,
    ex_ss,
    ex_rs,
    rs_ss,
    rs_rs,
    sec_ss,
    sec_rs,
    sc_ss,
    sc_rs,
    ag_ss,
    ag_rs,
    ql_ss,
    ql_rs,
):
    rows, D = partial.shape
    share = rows // T
    half = share // 2
    n_chunk = half // CHUNK
    cols = D // T
    rc = qshrink.shape[1]
    n_wide = D // WIDE
    t = lax.axis_index("tensor")
    sec = lax.axis_index("section")
    next_sec = lax.rem(sec + 1, S)
    prev_sec = lax.rem(sec + S - 1, S)
    h = t // 2
    p = h + lax.rem(t, 2) * (T - 1 - 2 * h)

    def at_ring(q):
        q = lax.rem(q + 2 * T, T)
        u = q // (T // 2)
        return (1 - u) * 2 * q + u * (2 * (T - 1 - q) + 1)

    to = (at_ring(p + 1), at_ring(p - 1))
    step_sign = (-1, 1)

    loads = [
        pltpu.make_async_copy(a, b, load_sem.at[i])
        for i, (a, b) in enumerate(
            (
                (hidden_in, hidden),
                (shrink_in, shrink),
                (up_in, up),
                (residual_in, residual),
                (qkv_in, qkv_w),
                (qshrink_in, qshrink),
                (expand_in, expand),
            )
        )
    ]

    def down_load(j):
        at = pl.ds(pl.multiple_of(j * WIDE, WIDE), WIDE)
        return pltpu.make_async_copy(down_in.at[:, at], down.at[:, at], down_sem.at[j])

    loads[0].start()
    loads[1].start()
    for j in range(n_wide):
        down_load(j).start()
    for load in loads[2:]:
        load.start()

    barrier = pltpu.get_barrier_semaphore()
    for k in range(1, T):
        pl.semaphore_signal(
            barrier, inc=1, device_id={"tensor": lax.rem(t + k, T)}, device_id_type=MESH
        )
    for other in (next_sec, prev_sec):
        pl.semaphore_signal(
            barrier, inc=1, device_id={"section": other}, device_id_type=MESH
        )

    loads[0].wait()
    loads[1].wait()
    low_mine[...] = (
        jnp.dot(hidden[...], shrink[...], preferred_element_type=F32)
        .astype(BF16)
        .reshape(low_mine.shape)
    )
    pl.semaphore_wait(barrier, T + 1)

    def low_copy(k):
        peer = lax.rem(t + k, T)
        return pltpu.make_async_remote_copy(
            src_ref=low_mine.at[peer],
            dst_ref=low_in.at[k],
            send_sem=low_ss.at[k],
            recv_sem=low_rs.at[k],
            device_id={"tensor": peer},
            device_id_type=MESH,
        )

    def dlow_copy(k, block):
        return pltpu.make_async_remote_copy(
            src_ref=dlow.at[block],
            dst_ref=dlow.at[block],
            send_sem=dlow_ss.at[k],
            recv_sem=dlow_rs.at[k],
            device_id={"tensor": lax.rem(t + k, T)},
            device_id_type=MESH,
        )

    for k in range(1, T):
        low_copy(k).start()

    scale_copy = pltpu.make_async_remote_copy(
        src_ref=scale_t_in,
        dst_ref=scale_t,
        send_sem=sc_ss.at[0],
        recv_sem=sc_rs.at[0],
        device_id={"section": next_sec},
        device_id_type=MESH,
    )
    scale_copy.start()

    def product(j, first, second):
        at = pl.ds(pl.multiple_of(j * WIDE, WIDE), WIDE)
        got = jnp.dot(lhs[...], down[:, at], preferred_element_type=F32).astype(BF16)
        partial[pl.ds(first, share), at] = got[:share]
        partial[pl.ds(second, share), at] = got[share:]

    def pair(i):
        a = at_ring(p - 1 - i)
        last = (i + 1) // (T // 2)
        b = at_ring(p + (i + 1) * (1 - last))
        return a, b

    def row_of(block):
        return pl.multiple_of(block * share, share)

    def fill(i):
        a, b = pair(i)
        lhs[:share] = hidden[pl.ds(row_of(a), share), :]
        lhs[share:] = hidden[pl.ds(row_of(b), share), :]
        return row_of(a), row_of(b)

    my_cols = pl.ds(pl.multiple_of(t * cols, cols), cols)

    def adapter_term(block):
        return jnp.dot(dlow[block], up[...], preferred_element_type=F32)

    def add_adapter(first, count, term):
        at = pl.ds(pl.multiple_of(first, CHUNK), count)
        partial[at, my_cols] = (partial[at, my_cols].astype(F32) + term).astype(BF16)

    def run_pass(i):
        first, second = fill(i)

        @pl.loop(0, n_wide)
        def _(j):
            product(j, first, second)

    first, second = fill(0)

    def early(j):
        down_load(j).wait()
        product(j, first, second)

    pl.loop(0, n_wide // 2)(early)
    total = low_mine[t].astype(F32)
    for k in range(1, T):
        low_copy(k).wait_recv()
        total = total + low_in[k].astype(F32)
    dlow[t] = (total * scale_ref[...]).astype(BF16)
    for k in range(1, T):
        dlow_copy(k, t).start()
    pl.loop(n_wide // 2, n_wide)(early)

    def rs_copy(d, c, s, src):
        return pltpu.make_async_remote_copy(
            src_ref=src,
            dst_ref=rs.at[d, s, c],
            send_sem=rs_ss.at[d, s, c],
            recv_sem=rs_rs.at[d, s, c],
            device_id={"tensor": to[d]},
            device_id_type=MESH,
        )

    def rows_at(d, c, block):
        return pl.ds(pl.multiple_of(block * share + (d * half + c * CHUNK), CHUNK), CHUNK)

    def in_share(d, c):
        return pl.ds(d * half + c * CHUNK, CHUNK)

    lanes = [(c, d) for c in range(n_chunk) for d in range(2)]
    for c, d in lanes:
        rs_copy(d, c, 0, partial.at[rows_at(d, c, at_ring(p + step_sign[d]))]).start()

    run_pass(1)
    loads[2].wait()
    for k in range(1, T):
        dlow_copy(k, lax.rem(t + T - k, T)).wait_recv()

    def ex_copy(d):
        return pltpu.make_async_remote_copy(
            src_ref=ex_out.at[d],
            dst_ref=ex_in.at[d],
            send_sem=ex_ss.at[d],
            recv_sem=ex_rs.at[d],
            device_id={"tensor": to[1 - d]},
            device_id_type=MESH,
        )

    before, after = at_ring(p - 1), at_ring(p + 1)
    term = adapter_term(before)
    ex_out[0] = term[:half].astype(BF16)
    add_adapter(before * share + half, half, term[half:])
    term = adapter_term(after)
    ex_out[1] = term[half:].astype(BF16)
    add_adapter(after * share, half, term[:half])
    for d in range(2):
        ex_copy(d).start()

    def terms_of(i):
        a, b = pair(i)
        add_adapter(row_of(a), share, adapter_term(a))
        add_adapter(row_of(b), share, adapter_term(b))

    terms_of(1)

    @pl.loop(0, T - 2)
    def _(s):
        for c, d in lanes:
            rs_copy(d, c, s, rs.at[d, s, c]).wait_recv()
            block = at_ring(p + step_sign[d] * (s + 2))
            rs[d, s, c] = (
                rs[d, s, c].astype(F32) + partial[rows_at(d, c, block), :].astype(F32)
            ).astype(BF16)
            rs_copy(d, c, s + 1, rs.at[d, s, c]).start()

        @pl.when(s + 2 < T // 2)
        def _():
            run_pass(s + 2)
            terms_of(s + 2)

    def sec_copy(d, c):
        return pltpu.make_async_remote_copy(
            src_ref=stream_ref.at[in_share(d, c)],
            dst_ref=arrived.at[in_share(d, c)],
            send_sem=sec_ss.at[d, c],
            recv_sem=sec_rs.at[d, c],
            device_id={"section": next_sec},
            device_id_type=MESH,
        )

    def ag_copy(d, c, s, block):
        return pltpu.make_async_remote_copy(
            src_ref=ag.at[rows_at(d, c, block)],
            dst_ref=ag.at[rows_at(d, c, block)],
            send_sem=ag_ss.at[d, s, c],
            recv_sem=ag_rs.at[d, s, c],
            device_id={"tensor": to[d]},
            device_id_type=MESH,
        )

    loads[3].wait()
    for d in range(2):
        ex_copy(d).wait_recv()
    for c, d in lanes:
        s = T - 2
        rs_copy(d, c, s, rs.at[d, s, c]).wait_recv()
        at = in_share(d, c)
        mine = rows_at(d, c, t)
        total = rs[d, s, c].astype(F32) + partial[mine, :].astype(F32)
        rs[d, s, c] = total.astype(BF16)
        stream_ref[at, :] = (total + residual[at, :].astype(F32)).astype(BF16)
        sender_cols = pl.ds(pl.multiple_of(at_ring(p - step_sign[d]) * cols, cols), cols)
        stream_ref[at, sender_cols] = (
            rs[d, s, c, :, sender_cols].astype(F32)
            + ex_in[d, pl.ds(c * CHUNK, CHUNK), :].astype(F32)
            + residual[at, sender_cols].astype(F32)
        ).astype(BF16)
        sec_copy(d, c).start()
    for c, d in lanes:
        at = in_share(d, c)
        sec_copy(d, c).wait_recv()
        values = arrived[at, :].astype(F32)
        inverse = lax.rsqrt(jnp.mean(values * values, axis=-1, keepdims=True) + 1e-05)
        ag[rows_at(d, c, t), :] = (values * inverse * gain_ref[...].astype(F32)).astype(BF16)
        ag_copy(d, c, 0, t).start()

    for load in loads[4:]:
        load.wait()
    qlow[...] = jnp.zeros_like(qlow)

    def multiply(a, b):
        at_a = pl.ds(pl.multiple_of(a * share, half), half)
        at_b = pl.ds(pl.multiple_of(b * share + half, half), half)
        lhs2[:half] = ag[at_a, :]
        lhs2[half:] = ag[at_b, :]
        low = jnp.dot(lhs2[...], qshrink[...], preferred_element_type=F32)
        qlow[at_a, :rc] = low[:half]
        qlow[at_b, :rc] = low[half:]

        def rest():
            got = jnp.dot(lhs2[...], qkv_w[...], preferred_element_type=F32)
            acc[at_a, :] = got[:half]
            acc[at_b, :] = got[half:]

        return rest

    multiply(t, t)()

    def gather_step(s, forward):
        for c, d in lanes:
            block = at_ring(p + step_sign[d] * (s + 1))
            ag_copy(d, c, s, block).wait_recv()
            if forward:
                ag_copy(d, c, s + 1, block).start()
        return multiply(at_ring(p - s - 1), at_ring(p + s + 1))

    @pl.loop(0, T - 2)
    def _(s):
        gather_step(s, True)()

    rest = gather_step(T - 2, False)
    scale_copy.wait()
    qlow_all[t] = (qlow[...].T[:rc] * scale_t[...]).astype(BF16)

    def ql_copy(k, block):
        return pltpu.make_async_remote_copy(
            src_ref=qlow_all.at[block],
            dst_ref=qlow_all.at[block],
            send_sem=ql_ss.at[k],
            recv_sem=ql_rs.at[k],
            device_id={"tensor": lax.rem(t + k, T)},
            device_id_type=MESH,
        )

    for k in range(1, T):
        ql_copy(k, t).start()
    rest()
    for k in range(1, T):
        ql_copy(k, lax.rem(t + T - k, T)).wait_recv()
    small = qlow_all[...].reshape(T * rc, rows)
    added = lax.dot_general(
        small, expand[...], (((0,), (0,)), ((), ())), preferred_element_type=F32
    )
    out_ref[...] = (acc[...] + added).astype(BF16)

    for k in range(1, T):
        low_copy(k).wait_send()
        dlow_copy(k, t).wait_send()
        ql_copy(k, t).wait_send()
    for d in range(2):
        ex_copy(d).wait_send()
        for c in range(n_chunk):
            sec_copy(d, c).wait_send()

            @pl.loop(0, T - 1)
            def _(s):
                rs_copy(d, c, s, rs.at[d, s, c]).wait_send()
                ag_copy(d, c, s, t).wait_send()


def per_device(
    T,
    S,
    hidden,
    down_weight,
    down_shrink,
    down_up_factors,
    residual,
    tenant_ids,
    adapter_rank,
    adapter_offset,
    norm_gain,
    qkv_weight,
    qkv_shrink,
    qkv_expand,
):
    rows, K = hidden.shape
    D = residual.shape[1]
    share = rows // T
    half = share // 2
    n_chunk = half // CHUNK
    R = down_shrink.shape[2]
    Q = qkv_weight.shape[2]
    rc = qkv_shrink.shape[2]
    cols = down_up_factors.shape[2]
    t = lax.axis_index("tensor")
    my_tenants = lax.dynamic_slice_in_dim(tenant_ids, t * share, share, 0)
    scale = adapter_scale(my_tenants, adapter_rank, adapter_offset, 0, R)
    scale_t = adapter_scale(tenant_ids, adapter_rank, adapter_offset, t * rc, rc).T

    any_spec = pl.BlockSpec(memory_space=pl.ANY)
    vmem = pl.BlockSpec(memory_space=pltpu.VMEM)
    dma = pltpu.SemaphoreType.DMA
    return pl.pallas_call(
        functools.partial(kernel, T, S),
        out_shape=(
            jax.ShapeDtypeStruct((share, D), BF16),
            jax.ShapeDtypeStruct((rows, Q), BF16),
        ),
        in_specs=[any_spec] * 5 + [vmem] + [any_spec] * 3 + [vmem] * 2,
        out_specs=(vmem, vmem),
        scratch_shapes=[
            pltpu.VMEM((rows, K), BF16),
            pltpu.VMEM((K, D), BF16),
            pltpu.VMEM((K, R), BF16),
            pltpu.VMEM((R, cols), BF16),
            pltpu.VMEM((share, D), BF16),
            pltpu.VMEM((D, Q), BF16),
            pltpu.VMEM((D, rc), BF16),
            pltpu.VMEM((R, Q), BF16),
            pltpu.VMEM((rows, D), BF16),
            pltpu.VMEM((2 * share, K), BF16),
            pltpu.VMEM((T, share, R), BF16),
            pltpu.VMEM((T, share, R), BF16),
            pltpu.VMEM((T, share, R), BF16),
            pltpu.VMEM((2, half, cols), BF16),
            pltpu.VMEM((2, half, cols), BF16),
            pltpu.VMEM((2, T - 1, n_chunk, CHUNK, D), BF16),
            pltpu.VMEM((share, D), BF16),
            pltpu.VMEM((rc, rows), F32),
            pltpu.VMEM((rows, D), BF16),
            pltpu.VMEM((share, D), BF16),
            pltpu.VMEM((rows, Q), F32),
            pltpu.VMEM((rows, 128), F32),
            pltpu.VMEM((T, rc, rows), BF16),
            dma((7,)),
            dma((D // WIDE,)),
            dma((T,)),
            dma((T,)),
            dma((T,)),
            dma((T,)),
            dma((2,)),
            dma((2,)),
            dma((2, T - 1, n_chunk)),
            dma((2, T - 1, n_chunk)),
            dma((2, n_chunk)),
            dma((2, n_chunk)),
            dma((1,)),
            dma((1,)),
            dma((2, T - 1, n_chunk)),
            dma((2, T - 1, n_chunk)),
            dma((T,)),
            dma((T,)),
        ],
        compiler_params=pltpu.CompilerParams(
            collective_id=0, has_side_effects=True, vmem_limit_bytes=60 * 1024 * 1024
        ),
        name="relay_boundary",
    )(
        hidden,
        down_weight[0],
        down_shrink[0],
        down_up_factors[0],
        residual,
        norm_gain,
        qkv_weight[0],
        qkv_shrink[0],
        qkv_expand[0],
        scale,
        scale_t,
    )


def solution(mesh):
    in_specs = (
        P("section", "tensor"),
        P("section", "tensor", None),
        P("section", "tensor", None),
        P("section", None, "tensor"),
        P(("section", "tensor"), None),
        P("section"),
        P(),
        P(),
        P("section", None),
        P("section", None, "tensor"),
        P("section", None, "tensor"),
        P("section", None, "tensor"),
    )
    out_specs = (P(("section", "tensor"), None), P("section", "tensor"))
    body = functools.partial(per_device, mesh.shape["tensor"], mesh.shape["section"])
    return jax.shard_map(
        body, mesh=mesh, in_specs=in_specs, out_specs=out_specs, check_vma=False
    )
```

time: 362 us -> 123 us (0.34)
  waiting for transfers between devices: 285 us -> 0 us
  Pallas kernels: 0 us -> 112 us
  blocking collectives: 30.7 us -> 0 us
  matrix products: 28.1 us -> 0 us
  between operations: 13.9 us -> 0.67 us
  local copies, waits for them, and re-layouts: 2.13 us -> 6.89 us
    all_gather x2 -> x0, waiting for transfers between devices: 123 us -> none  [the longest x1 70.1 us: per_device(): complete_rows = lax.all_gather(normed, 'tensor', axis=0, tiled=True)]
    pallas_call x0 -> x1, Pallas kernels: none -> 112 us  [per_device(): pl.pallas_call(functools.partial(kernel, T, S), out_shape=(jax.ShapeDtype...]
    reduce_scatter x1 -> x0, waiting for transfers between devices: 90.4 us -> none  [per_device(): lax.psum_scatter(rounded(jnp.dot(hidden, down_matrix, preferred_element_t...]
    psum x1 -> x0, waiting for transfers between devices: 59.9 us -> none  [per_device(): lax.psum(rounded(jnp.dot(hidden, down_factor, preferred_element_type=jnp....]
    all_gather x1 -> x0, blocking collectives: 30.7 us -> none  [per_device(): small_all = lax.all_gather(scaled_part, 'tensor', axis=1, tiled=True)]
    dot_general x6 -> x0, matrix products: 28.1 us -> none  [the longest x1 12.4 us: per_device(): jnp.dot(hidden, down_matrix, preferred_element_type=jnp.float32)]
    ppermute x2 -> x0, waiting for transfers between devices: 11.5 us -> none  [passed_along(): return lax.ppermute(block, axis, route)]
    unnamed x20 -> x3, local copies, waits for them, and re-layouts: 2.05 us -> 6.13 us
  transfers between devices with their start and end apart: 6 -> 0, of which waited for: 6 -> 0; matrix products, arithmetic and copies ran while one was open for 4% -> 0% of each run, Pallas kernels for 0% -> 0%
where the time goes in v1:
time: 123 us; the launch traced here: 122 us
  Pallas kernels  112 us (91%)
  local copies, waits for them, and re-layouts  6.89 us (6%)
  other arithmetic  2.99 us (2%)
    pallas_call x1, Pallas kernels, per_device(): pl.pallas_call(functools.partial(kernel, T, S), out_shape=(jax.ShapeDtype...  112 us
    unnamed x3, local copies, waits for them, and re-layouts  6.13 us

profile of v1, /device:TPU:0, one launch (start us, length us, event | category | flops | bytes accessed | tf_op | source)
XLA Modules:
  0.0 122.3 jit_solution(17188374648904285743)
XLA Ops:
  0.6 0.8 dynamic_slice.3
  1.4 0.8 select_reduce_fusion.3
  2.2 0.8 select_reduce_fusion.1
  3.0 0.7 and_select_fusion.scale_t_in
  3.7 0.7 fusion.1.scale_ref
  4.4 2.3 %copy.15 = bf16[1,4096,32]{2,1,0:T(8,128)(2,1)} copy(bf16[1,4096,32]{1,2,0:T(8,128)(2,1)} %param.22) | data formatting | bytes 524288 | tf_op args[10]
  6.7 111.8 %relay_boundary.1 = (bf16[64,4096]{1,0:T(8,128)(2,1)}, bf16[512,640]{1,0:T(8,128)(2,1)}) custom-call(bf16[512,1792]{1,0:T(8,128)(2,1)} %hidden_in.1, bf16[1792,4096]{1,0:T(8,128)(2,1)} %bitcast.6, bf16[1792,256]{1,0:T(8,128)(2,1)} %bitcast.9, bf16[256,512]{1,0:T(8,128)(2,1)} %bitcast.11, bf16[64,4096]{1,0:T(8,128)(2,1)} %residual_in.1, ...), custom_call_target="tpu_custom_call" | custom-call | tf_op jit(solution)/shard_map/relay_boundary/pallas_call | solution.py:466
  118.5 1.9 %copy.18 = bf16[64,4096]{1,0:T(8,128)(2,1)} copy(bf16[64,4096]{1,0:T(8,128)(2,1)} %get-tuple-element.8) | data formatting | bytes 1048576
  120.4 2.0 %copy.19 = bf16[512,640]{1,0:T(8,128)(2,1)} copy(bf16[512,640]{1,0:T(8,128)(2,1)} %get-tuple-element.9) | data formatting | bytes 1310720
  (5 shorter events, 0.0 us)

commit v2 on v1

v2 whole, which is shorter than its diff:
```python
import functools

import jax
import jax.numpy as jnp
from jax import lax
from jax.experimental import pallas as pl
from jax.experimental.pallas import tpu as pltpu
from jax.sharding import PartitionSpec as P

adapter_alpha_scale = 32.0
MESH = pl.DeviceIdType.MESH
F32 = jnp.float32
BF16 = jnp.bfloat16
CHUNK = 16
WIDE = 512


def kernel(
    T,
    S,
    hidden_in,
    down_in,
    shrink_in,
    up_in,
    residual_in,
    gain_ref,
    qkv_in,
    qshrink_in,
    expand_in,
    ids_ref,
    rank_ref,
    offset_ref,
    stream_ref,
    out_ref,
    hidden,
    down,
    shrink,
    up,
    residual,
    qkv_w,
    qshrink,
    expand,
    partial,
    lhs,
    low_mine,
    low_in,
    dlow,
    ex_out,
    ex_in,
    rs,
    arrived,
    scale_t,
    scale_all,
    scale_rows,
    ag,
    lhs2,
    acc,
    qlow,
    qlow_all,
    load_sem,
    down_sem,
    low_ss,
    low_rs,
    dlow_ss,
    dlow_rs,
    ex_ss,
    ex_rs,
    rs_ss,
    rs_rs,
    sec_ss,
    sec_rs,
    sc_ss,
    sc_rs,
    ag_ss,
    ag_rs,
    ql_ss,
    ql_rs,
):
    rows, D = partial.shape
    share = rows // T
    half = share // 2
    n_chunk = half // CHUNK
    cols = D // T
    rc = qshrink.shape[0]
    n_wide = D // WIDE
    t = lax.axis_index("tensor")
    sec = lax.axis_index("section")
    next_sec = lax.rem(sec + 1, S)
    prev_sec = lax.rem(sec + S - 1, S)
    h = t // 2
    p = h + lax.rem(t, 2) * (T - 1 - 2 * h)

    def at_ring(q):
        q = lax.rem(q + 2 * T, T)
        u = q // (T // 2)
        return (1 - u) * 2 * q + u * (2 * (T - 1 - q) + 1)

    to = (at_ring(p + 1), at_ring(p - 1))
    sign = (1, -1)
    far = T // 2
    all_chunks = 2 * n_chunk
    first_half, second_half = range(n_chunk), range(n_chunk, all_chunks)
    mixed = [c for pair_of in zip(second_half, first_half) for c in pair_of]
    swapped = [c for pair_of in zip(first_half, second_half) for c in pair_of]
    whole_way = (first_half, second_half)
    one_less = (second_half, first_half)

    loads = [
        pltpu.make_async_copy(a, b, load_sem.at[i])
        for i, (a, b) in enumerate(
            (
                (hidden_in, hidden),
                (shrink_in, shrink),
                (up_in, up),
                (residual_in, residual),
                (qkv_in, qkv_w),
                (qshrink_in, qshrink),
                (expand_in, expand),
            )
        )
    ]

    def down_load(j):
        at = pl.ds(pl.multiple_of(j * WIDE, WIDE), WIDE)
        return pltpu.make_async_copy(down_in.at[:, at], down.at[:, at], down_sem.at[j])

    loads[0].start()
    loads[1].start()
    for j in range(n_wide):
        down_load(j).start()
    for load in loads[2:]:
        load.start()

    barrier = pltpu.get_barrier_semaphore()
    for k in range(1, T):
        pl.semaphore_signal(
            barrier, inc=1, device_id={"tensor": lax.rem(t + k, T)}, device_id_type=MESH
        )
    for other in (next_sec, prev_sec):
        pl.semaphore_signal(
            barrier, inc=1, device_id={"section": other}, device_id_type=MESH
        )

    ids = ids_ref[...]
    lower = jnp.zeros_like(ids)
    ranks = jnp.zeros_like(ids)
    for k in range(rank_ref.shape[0]):
        lower = lower + jnp.where(ids == k, offset_ref[k], 0)
        ranks = ranks + jnp.where(ids == k, rank_ref[k], 0)
    column = lax.broadcasted_iota(jnp.int32, scale_all.shape, 0)
    inside = (column >= lower) & (column < lower + ranks)
    scale_all[...] = jnp.where(inside, adapter_alpha_scale / ranks.astype(F32), 0.0)
    scale_rows[...] = scale_all[...].T

    loads[0].wait()
    loads[1].wait()
    low_mine[...] = (
        jnp.dot(hidden[...], shrink[...], preferred_element_type=F32)
        .astype(BF16)
        .reshape(low_mine.shape)
    )
    pl.semaphore_wait(barrier, T + 1)

    def low_copy(k):
        peer = lax.rem(t + k, T)
        return pltpu.make_async_remote_copy(
            src_ref=low_mine.at[peer],
            dst_ref=low_in.at[k],
            send_sem=low_ss.at[k],
            recv_sem=low_rs.at[k],
            device_id={"tensor": peer},
            device_id_type=MESH,
        )

    def dlow_copy(k, block):
        return pltpu.make_async_remote_copy(
            src_ref=dlow.at[block],
            dst_ref=dlow.at[block],
            send_sem=dlow_ss.at[k],
            recv_sem=dlow_rs.at[k],
            device_id={"tensor": lax.rem(t + k, T)},
            device_id_type=MESH,
        )

    for k in range(1, T):
        low_copy(k).start()

    scale_copy = pltpu.make_async_remote_copy(
        src_ref=scale_all.at[pl.ds(pl.multiple_of(t * rc, rc), rc)],
        dst_ref=scale_t,
        send_sem=sc_ss.at[0],
        recv_sem=sc_rs.at[0],
        device_id={"section": next_sec},
        device_id_type=MESH,
    )
    scale_copy.start()

    def product(j, first, second):
        at = pl.ds(pl.multiple_of(j * WIDE, WIDE), WIDE)
        got = jnp.dot(lhs[...], down[:, at], preferred_element_type=F32).astype(BF16)
        partial[pl.ds(first, share), at] = got[:share]
        partial[pl.ds(second, share), at] = got[share:]

    def pair(i):
        return at_ring(p + far - i), (t if i == 0 else at_ring(p - far + i))

    def row_of(block):
        return pl.multiple_of(block * share, share)

    def fill(i):
        a, b = pair(i)
        lhs[:share] = hidden[pl.ds(row_of(a), share), :]
        lhs[share:] = hidden[pl.ds(row_of(b), share), :]
        return row_of(a), row_of(b)

    my_cols = pl.ds(pl.multiple_of(t * cols, cols), cols)

    def adapter_term(block):
        return jnp.dot(dlow[block], up[...], preferred_element_type=F32)

    def add_adapter(first, count, term):
        at = pl.ds(pl.multiple_of(first, CHUNK), count)
        partial[at, my_cols] = (partial[at, my_cols].astype(F32) + term).astype(BF16)

    def run_pass(i):
        first, second = fill(i)

        @pl.loop(0, n_wide)
        def _(j):
            product(j, first, second)

    first, second = fill(0)

    def early(j):
        down_load(j).wait()
        product(j, first, second)

    pl.loop(0, n_wide // 2)(early)
    total = low_mine[t].astype(F32)
    for k in range(1, T):
        low_copy(k).wait_recv()
        total = total + low_in[k].astype(F32)
    dlow[t] = (total * scale_rows[pl.ds(row_of(t), share), :]).astype(BF16)
    for k in range(1, T):
        dlow_copy(k, t).start()
    pl.loop(n_wide // 2, n_wide)(early)

    def rs_copy(d, c, k, src):
        return pltpu.make_async_remote_copy(
            src_ref=src,
            dst_ref=rs.at[d, k - 1, c],
            send_sem=rs_ss.at[d, k - 1, c],
            recv_sem=rs_rs.at[d, k - 1, c],
            device_id={"tensor": to[d]},
            device_id_type=MESH,
        )

    def rows_at(c, block):
        return pl.ds(pl.multiple_of(block * share + c * CHUNK, CHUNK), CHUNK)

    def in_share(c):
        return pl.ds(c * CHUNK, CHUNK)

    def begin(d, c, k):
        rs_copy(d, c, k, partial.at[rows_at(c, at_ring(p + sign[d] * k))]).start()

    def ex_copy(d):
        return pltpu.make_async_remote_copy(
            src_ref=ex_out.at[d],
            dst_ref=ex_in.at[d],
            send_sem=ex_ss.at[d],
            recv_sem=ex_rs.at[d],
            device_id={"tensor": to[d]},
            device_id_type=MESH,
        )

    def pass_on(d, c, k):
        slot = rs.at[d, k, c]
        rs_copy(d, c, k + 1, slot).wait_recv()
        here = rows_at(c, at_ring(p + sign[d] * k))
        if k + 1 == far:
            sender_cols = pl.ds(pl.multiple_of(at_ring(p - sign[d]) * cols, cols), cols)
            late = ex_in[d, pl.ds((c - d * n_chunk) * CHUNK, CHUNK), :].astype(F32)
            slot[:, sender_cols] = (slot[:, sender_cols].astype(F32) + late).astype(BF16)
        slot[...] = (slot[...].astype(F32) + partial[here, :].astype(F32)).astype(BF16)
        rs_copy(d, c, k, slot).start()

    for i in range(n_chunk):
        for d in range(2):
            begin(d, whole_way[d][i], far)

    run_pass(1)
    loads[2].wait()
    for k in range(1, T):
        dlow_copy(k, lax.rem(t + T - k, T)).wait_recv()

    def add_terms(block):
        term = jnp.dot(dlow[block], up[...], preferred_element_type=F32)
        at = pl.ds(row_of(block), share)
        partial[at, my_cols] = (partial[at, my_cols].astype(F32) + term).astype(BF16)

    term = jnp.dot(dlow[at_ring(p + far)], up[...], preferred_element_type=F32)
    ex_out[0] = term[:half].astype(BF16)
    ex_out[1] = term[half:].astype(BF16)
    for d in range(2):
        ex_copy(d).start()

    def terms_of(i):
        for block in pair(i):
            add_terms(block)

    terms_of(1)
    for i in range(n_chunk):
        for d in range(2):
            begin(d, one_less[d][i], far - 1)
    if far > 2:
        run_pass(2)
        terms_of(2)
    for d in range(2):
        ex_copy(d).wait_recv()
    for i in range(n_chunk):
        for d in range(2):
            pass_on(d, whole_way[d][i], far - 1)
    for k in range(far - 2, 0, -1):
        if far - k > 2:
            run_pass(far - k)
            terms_of(far - k)
        for i in range(all_chunks):
            for d in range(2):
                pass_on(d, (mixed if d == 0 or k == 1 else swapped)[i], k)
    add_terms(t)

    def sec_copy(c):
        return pltpu.make_async_remote_copy(
            src_ref=stream_ref.at[in_share(c)],
            dst_ref=arrived.at[in_share(c)],
            send_sem=sec_ss.at[c],
            recv_sem=sec_rs.at[c],
            device_id={"section": next_sec},
            device_id_type=MESH,
        )

    def ag_copy(d, c, hop, block):
        return pltpu.make_async_remote_copy(
            src_ref=ag.at[rows_at(c, block)],
            dst_ref=ag.at[rows_at(c, block)],
            send_sem=ag_ss.at[d, hop, c],
            recv_sem=ag_rs.at[d, hop, c],
            device_id={"tensor": to[d]},
            device_id_type=MESH,
        )

    loads[3].wait()

    def finish(c):
        at = in_share(c)
        total = partial[rows_at(c, t), :].astype(F32) + residual[at, :].astype(F32)
        for d in range(2):
            rs_copy(d, c, 1, rs.at[d, 0, c]).wait_recv()
            total = total + rs[d, 0, c].astype(F32)
        stream_ref[at, :] = total.astype(BF16)
        sec_copy(c).start()

    def normalise(c):
        sec_copy(c).wait_recv()
        values = arrived[in_share(c), :].astype(F32)
        inverse = lax.rsqrt(jnp.mean(values * values, axis=-1, keepdims=True) + 1e-05)
        ag[rows_at(c, t), :] = (values * inverse * gain_ref[...].astype(F32)).astype(BF16)
        for d in range(2):
            ag_copy(d, c, 0, t).start()

    for i, c in enumerate(mixed):
        finish(c)
        if i:
            normalise(mixed[i - 1])
    normalise(mixed[-1])

    for load in loads[4:]:
        load.wait()
    qlow[...] = jnp.zeros_like(qlow)

    NT = (((1,), (1,)), ((), ()))

    def multiply(blocks):
        count = len(blocks) * share
        for i, block in enumerate(blocks):
            lhs2[pl.ds(i * share, share), :] = ag[pl.ds(row_of(block), share), :]
        low = lax.dot_general(lhs2[:count], qshrink[...], NT, preferred_element_type=F32)
        for i, block in enumerate(blocks):
            qlow[pl.ds(row_of(block), share), :rc] = low[i * share : (i + 1) * share]

        def rest():
            got = jnp.dot(lhs2[:count], qkv_w[...], preferred_element_type=F32)
            for i, block in enumerate(blocks):
                acc[pl.ds(row_of(block), share), :] = got[i * share : (i + 1) * share]

        return rest

    multiply([t])()
    for hop in range(far - 1):
        for c in mixed:
            for d in range(2):
                block = at_ring(p - sign[d] * (hop + 1))
                ag_copy(d, c, hop, block).wait_recv()
                if hop + 1 < far - 1 or c in whole_way[d]:
                    ag_copy(d, c, hop + 1, block).start()
        multiply([at_ring(p - hop - 1), at_ring(p + hop + 1)])()
    opposite = at_ring(p + far)
    for d in range(2):
        for c in whole_way[d]:
            ag_copy(d, c, far - 1, opposite).wait_recv()
    rest = multiply([opposite])
    scale_copy.wait()
    qlow_all[t] = (qlow[...].T[:rc] * scale_t[...]).astype(BF16)

    def ql_copy(k, block):
        return pltpu.make_async_remote_copy(
            src_ref=qlow_all.at[block],
            dst_ref=qlow_all.at[block],
            send_sem=ql_ss.at[k],
            recv_sem=ql_rs.at[k],
            device_id={"tensor": lax.rem(t + k, T)},
            device_id_type=MESH,
        )

    for k in range(1, T):
        ql_copy(k, t).start()
    rest()
    for k in range(1, T):
        ql_copy(k, lax.rem(t + T - k, T)).wait_recv()
    small = qlow_all[...].reshape(T * rc, rows)
    added = lax.dot_general(
        small, expand[...], (((0,), (0,)), ((), ())), preferred_element_type=F32
    )
    out_ref[...] = (acc[...] + added).astype(BF16)

    for k in range(1, T):
        low_copy(k).wait_send()
        dlow_copy(k, t).wait_send()
        ql_copy(k, t).wait_send()
    for c in range(all_chunks):
        sec_copy(c).wait_send()
    for d in range(2):
        ex_copy(d).wait_send()
        for c in range(all_chunks):
            for k in range(far if c in whole_way[d] else far - 1):
                rs_copy(d, c, k + 1, rs.at[d, k, c]).wait_send()
                ag_copy(d, c, k, t).wait_send()


def copy_out(stream_in, out_in, stream_ref, out_ref, sem):
    copies = [
        pltpu.make_async_copy(stream_in, stream_ref, sem.at[0]),
        pltpu.make_async_copy(out_in, out_ref, sem.at[1]),
    ]
    for copy in copies:
        copy.start()
    for copy in copies:
        copy.wait()


def per_device(
    T,
    S,
    hidden,
    down_weight,
    down_shrink,
    down_up_factors,
    residual,
    tenant_ids,
    adapter_rank,
    adapter_offset,
    norm_gain,
    qkv_weight,
    qkv_shrink,
    qkv_expand,
):
    rows, K = hidden.shape
    D = residual.shape[1]
    share = rows // T
    half = share // 2
    R = down_shrink.shape[2]
    Q = qkv_weight.shape[2]
    rc = qkv_shrink.shape[2]
    cols = down_up_factors.shape[2]
    any_spec = pl.BlockSpec(memory_space=pl.ANY)
    vmem = pl.BlockSpec(memory_space=pltpu.VMEM)
    dma = pltpu.SemaphoreType.DMA
    smem = pl.BlockSpec(memory_space=pltpu.SMEM)
    outs = pl.pallas_call(
        functools.partial(kernel, T, S),
        out_shape=(
            pltpu.VMEM((share, D), BF16),
            pltpu.VMEM((rows, Q), BF16),
        ),
        in_specs=[any_spec] * 5 + [vmem] + [any_spec] * 3 + [vmem, smem, smem],
        out_specs=(vmem, vmem),
        scratch_shapes=[
            pltpu.VMEM((rows, K), BF16),
            pltpu.VMEM((K, D), BF16),
            pltpu.VMEM((K, R), BF16),
            pltpu.VMEM((R, cols), BF16),
            pltpu.VMEM((share, D), BF16),
            pltpu.VMEM((D, Q), BF16),
            pltpu.VMEM((rc, D), BF16),
            pltpu.VMEM((R, Q), BF16),
            pltpu.VMEM((rows, D), BF16),
            pltpu.VMEM((2 * share, K), BF16),
            pltpu.VMEM((T, share, R), BF16),
            pltpu.VMEM((T, share, R), BF16),
            pltpu.VMEM((T, share, R), BF16),
            pltpu.VMEM((2, half, cols), BF16),
            pltpu.VMEM((2, half, cols), BF16),
            pltpu.VMEM((2, T // 2, share // CHUNK, CHUNK, D), BF16),
            pltpu.VMEM((share, D), BF16),
            pltpu.VMEM((rc, rows), F32),
            pltpu.VMEM((R, rows), F32),
            pltpu.VMEM((rows, R), F32),
            pltpu.VMEM((rows, D), BF16),
            pltpu.VMEM((2 * share, D), BF16),
            pltpu.VMEM((rows, Q), F32),
            pltpu.VMEM((rows, 128), F32),
            pltpu.VMEM((T, rc, rows), BF16),
            dma((7,)),
            dma((D // WIDE,)),
            dma((T,)),
            dma((T,)),
            dma((T,)),
            dma((T,)),
            dma((2,)),
            dma((2,)),
            dma((2, T // 2, share // CHUNK)),
            dma((2, T // 2, share // CHUNK)),
            dma((share // CHUNK,)),
            dma((share // CHUNK,)),
            dma((1,)),
            dma((1,)),
            dma((2, T // 2, share // CHUNK)),
            dma((2, T // 2, share // CHUNK)),
            dma((T,)),
            dma((T,)),
        ],
        compiler_params=pltpu.CompilerParams(
            collective_id=0, has_side_effects=True, vmem_limit_bytes=61 * 1024 * 1024
        ),
        name="relay_boundary",
    )(
        hidden,
        down_weight[0],
        down_shrink[0],
        down_up_factors[0],
        residual,
        norm_gain,
        qkv_weight[0],
        qkv_shrink[0].T,
        qkv_expand[0],
        tenant_ids.reshape(1, rows),
        adapter_rank,
        adapter_offset,
    )
    return pl.pallas_call(
        copy_out,
        out_shape=tuple(jax.ShapeDtypeStruct(o.shape, o.dtype) for o in outs),
        in_specs=[vmem] * 2,
        out_specs=(any_spec, any_spec),
        scratch_shapes=[dma((2,))],
        name="copy_out",
    )(*outs)


def solution(mesh):
    in_specs = (
        P("section", "tensor"),
        P("section", "tensor", None),
        P("section", "tensor", None),
        P("section", None, "tensor"),
        P(("section", "tensor"), None),
        P("section"),
        P(),
        P(),
        P("section", None),
        P("section", None, "tensor"),
        P("section", None, "tensor"),
        P("section", None, "tensor"),
    )
    out_specs = (P(("section", "tensor"), None), P("section", "tensor"))
    body = functools.partial(per_device, mesh.shape["tensor"], mesh.shape["section"])
    return jax.shard_map(
        body, mesh=mesh, in_specs=in_specs, out_specs=out_specs, check_vma=False
    )
```

time: 123 us -> 113 us (0.919)
  local copies, waits for them, and re-layouts: 6.89 us -> 1.61 us
  other arithmetic: 2.99 us -> 0 us
  Pallas kernels: 112 us -> 110 us
    unnamed x3 -> x4, local copies, waits for them, and re-layouts: 6.13 us -> 1.61 us
    reduce_sum x2 -> x0, other arithmetic: 1.53 us -> none  [table_lookup(): return jnp.sum(jnp.where(chosen, table[None, :], 0), axis=1)]
    select_n x2 -> x0, other arithmetic: 1.43 us -> none  [adapter_scale(): return jnp.where(inside, scaling_factor[:, None], jnp.float32(0.0))]
    pallas_call x1 -> x2, Pallas kernels: 112 us -> 110 us  [the longest x1 108 us: per_device(): pl.pallas_call(functools.partial(kernel, T, S), out_shape=(pltpu.VMEM((sh...]
where the time goes in v2:
time: 113 us
  Pallas kernels  110 us (97%)
  local copies, waits for them, and re-layouts  1.61 us (1%)
    pallas_call x1, Pallas kernels, per_device(): pl.pallas_call(functools.partial(kernel, T, S), out_shape=(pltpu.VMEM((sh...  108 us
    pallas_call x1, Pallas kernels, per_device(): pl.pallas_call(copy_out, out_shape=tuple((jax.ShapeDtypeStruct(o.shape, o...  2.27 us

profile of v2, /device:TPU:0, one launch (start us, length us, event | category | flops | bytes accessed | tf_op | source)
XLA Modules:
  0.0 112.6 jit_solution(11292205810745824172)
XLA Ops:
  0.6 108.1 %relay_boundary.1 = (bf16[64,4096]{1,0:T(8,128)(2,1)S(1)}, bf16[512,640]{1,0:T(8,128)(2,1)S(1)}) custom-call(bf16[512,1792]{1,0:T(8,128)(2,1)} %hidden_in.1, bf16[1792,4096]{1,0:T(8,128)(2,1)} %bitcast.9, bf16[1792,256]{1,0:T(8,128)(2,1)} %bitcast.11, bf16[256,512]{1,0:T(8,128)(2,1)} %bitcast.13, bf16[64,4096]{1,0:T(8,128)(2,1)} %residual_in.1, ...), custom_call_target="tpu_custom_call" | custom-call | tf_op jit(solution)/shard_map/relay_boundary/pallas_call | solution.py:490
  108.7 0.0 copy-start
  108.8 0.8 copy-done
  109.6 0.0 copy-start.1
  109.6 0.8 copy-done.1
  110.4 2.3 %copy_out.1 = (bf16[64,4096]{1,0:T(8,128)(2,1)}, bf16[512,640]{1,0:T(8,128)(2,1)}) custom-call(bf16[64,4096]{1,0:T(8,128)(2,1)} %copy-done.1, bf16[512,640]{1,0:T(8,128)(2,1)} %copy-done), custom_call_target="tpu_custom_call" | custom-call | tf_op jit(solution)/shard_map/copy_out/pallas_call | solution.py:561
Async XLA Ops:
  108.7 0.8 copy-start
  109.6 0.8 copy-start.1

commit v3 on v2

--- a/solution.py
+++ b/solution.py
@@ -105,31 +105,41 @@
     whole_way = (first_half, second_half)
     one_less = (second_half, first_half)
 
-    loads = [
-        pltpu.make_async_copy(a, b, load_sem.at[i])
-        for i, (a, b) in enumerate(
-            (
-                (hidden_in, hidden),
-                (shrink_in, shrink),
-                (up_in, up),
-                (residual_in, residual),
-                (qkv_in, qkv_w),
-                (qshrink_in, qshrink),
-                (expand_in, expand),
+    def pieces(source, target, sem, count):
+        size = target.shape[0] // count
+        return [
+            pltpu.make_async_copy(
+                source.at[pl.ds(i * size, size)], target.at[pl.ds(i * size, size)], sem
             )
-        )
-    ]
-
-    def down_load(j):
+            for i in range(count)
+        ]
+
+    wide_k = down.shape[0] // 4
+
+    def down_load(j, first, size):
         at = pl.ds(pl.multiple_of(j * WIDE, WIDE), WIDE)
-        return pltpu.make_async_copy(down_in.at[:, at], down.at[:, at], down_sem.at[j])
-
-    loads[0].start()
-    loads[1].start()
+        part = pl.ds(first, size)
+        return pltpu.make_async_copy(down_in.at[part, at], down.at[part, at], down_sem.at[j])
+
+    arrays = (
+        (hidden_in, hidden, 8),
+        (shrink_in, shrink, 4),
+        (up_in, up, 1),
+        (residual_in, residual, 1),
+        (qkv_in, qkv_w, 4),
+        (qshrink_in, qshrink, 1),
+        (expand_in, expand, 1),
+    )
+    loads = [pltpu.make_async_copy(x, y, load_sem.at[i]) for i, (x, y, n) in enumerate(arrays)]
+    parts = [pieces(x, y, load_sem.at[i], n) for i, (x, y, n) in enumerate(arrays)]
+    for copy in parts[0] + parts[1]:
+        copy.start()
     for j in range(n_wide):
-        down_load(j).start()
-    for load in loads[2:]:
-        load.start()
+        for i in range(4):
+            down_load(j, i * wide_k, wide_k).start()
+    for copies in parts[2:]:
+        for copy in copies:
+            copy.start()
 
     barrier = pltpu.get_barrier_semaphore()
     for k in range(1, T):
@@ -229,10 +239,13 @@
         def _(j):
             product(j, first, second)
 
+    def rows_at(c, block):
+        return pl.ds(pl.multiple_of(block * share + c * CHUNK, CHUNK), CHUNK)
+
     first, second = fill(0)
 
     def early(j):
-        down_load(j).wait()
+        down_load(j, 0, down.shape[0]).wait()
         product(j, first, second)
 
     pl.loop(0, n_wide // 2)(early)
@@ -254,9 +267,6 @@
             device_id={"tensor": to[d]},
             device_id_type=MESH,
         )
-
-    def rows_at(c, block):
-        return pl.ds(pl.multiple_of(block * share + c * CHUNK, CHUNK), CHUNK)
 
     def in_share(c):
         return pl.ds(c * CHUNK, CHUNK)
@@ -313,19 +323,19 @@
     for i in range(n_chunk):
         for d in range(2):
             begin(d, one_less[d][i], far - 1)
-    if far > 2:
-        run_pass(2)
-        terms_of(2)
     for d in range(2):
         ex_copy(d).wait_recv()
     for i in range(n_chunk):
         for d in range(2):
             pass_on(d, whole_way[d][i], far - 1)
+    if far > 2:
+        run_pass(2)
+        terms_of(2)
     for k in range(far - 2, 0, -1):
-        if far - k > 2:
-            run_pass(far - k)
-            terms_of(far - k)
         for i in range(all_chunks):
+            if i == n_chunk and k > 1:
+                run_pass(far - k + 1)
+                terms_of(far - k + 1)
             for d in range(2):
                 pass_on(d, (mixed if d == 0 or k == 1 else swapped)[i], k)
     add_terms(t)
@@ -429,10 +439,12 @@
     for k in range(1, T):
         ql_copy(k, lax.rem(t + T - k, T)).wait_recv()
     small = qlow_all[...].reshape(T * rc, rows)
-    added = lax.dot_general(
-        small, expand[...], (((0,), (0,)), ((), ())), preferred_element_type=F32
-    )
-    out_ref[...] = (acc[...] + added).astype(BF16)
+    for i in range(rows // 128):
+        at = slice(i * 128, (i + 1) * 128)
+        added = lax.dot_general(
+            small[:, at], expand[...], (((0,), (0,)), ((), ())), preferred_element_type=F32
+        )
+        out_ref[at, :] = (acc[at, :] + added).astype(BF16)
 
     for k in range(1, T):
         low_copy(k).wait_send()
@@ -443,16 +455,22 @@
     for d in range(2):
         ex_copy(d).wait_send()
         for c in range(all_chunks):
-            for k in range(far if c in whole_way[d] else far - 1):
+            for k in range(far - 1):
                 rs_copy(d, c, k + 1, rs.at[d, k, c]).wait_send()
                 ag_copy(d, c, k, t).wait_send()
+        for i in range(n_chunk):
+            ag_copy(d, whole_way[d][i], far - 1, t).wait_send()
+            rs_copy(d, whole_way[d][i], far, rs.at[d, far - 1, 0]).wait_send()
 
 
 def copy_out(stream_in, out_in, stream_ref, out_ref, sem):
-    copies = [
-        pltpu.make_async_copy(stream_in, stream_ref, sem.at[0]),
-        pltpu.make_async_copy(out_in, out_ref, sem.at[1]),
-    ]
+    copies = []
+    for source, target, size in ((out_in, out_ref, 64), (stream_in, stream_ref, CHUNK)):
+        for first in range(0, source.shape[0], size):
+            at = pl.ds(first, size)
+            copies.append(
+                pltpu.make_async_copy(source.at[at], target.at[at], sem.at[len(copies)])
+            )
     for copy in copies:
         copy.start()
     for copy in copies:
@@ -561,9 +579,9 @@
     return pl.pallas_call(
         copy_out,
         out_shape=tuple(jax.ShapeDtypeStruct(o.shape, o.dtype) for o in outs),
-        in_specs=[vmem] * 2,
+        in_specs=[any_spec] * 2,
         out_specs=(any_spec, any_spec),
-        scratch_shapes=[dma((2,))],
+        scratch_shapes=[dma((rows // 64 + share // CHUNK,))],
         name="copy_out",
     )(*outs)
 

time: 113 us -> 150 us (1.33)
  Pallas kernels: 110 us -> 147 us
    pallas_call x1, Pallas kernels: 2.27 us -> 36.9 us  [per_device(): pl.pallas_call(copy_out, out_shape=tuple((jax.ShapeDtypeStruct(o.shape, o...]
    pallas_call x1, Pallas kernels: 108 us -> 110 us  [per_device(): pl.pallas_call(functools.partial(kernel, T, S), out_shape=(pltpu.VMEM((sh...]
where the time goes in v3:
time: 150 us; the launch traced here: 149 us
  Pallas kernels  147 us (98%)
  local copies, waits for them, and re-layouts  1.61 us (1%)
    pallas_call x1, Pallas kernels, per_device(): pl.pallas_call(functools.partial(kernel, T, S), out_shape=(pltpu.VMEM((sh...  110 us
    pallas_call x1, Pallas kernels, per_device(): pl.pallas_call(copy_out, out_shape=tuple((jax.ShapeDtypeStruct(o.shape, o...  36.9 us

profile of v3, /device:TPU:0, one launch (start us, length us, event | category | flops | bytes accessed | tf_op | source)
XLA Modules:
  0.0 149.3 jit_solution(14245994366587604759)
XLA Ops:
  0.6 110.1 %relay_boundary.1 = (bf16[64,4096]{1,0:T(8,128)(2,1)S(1)}, bf16[512,640]{1,0:T(8,128)(2,1)S(1)}) custom-call(bf16[512,1792]{1,0:T(8,128)(2,1)} %hidden_in.1, bf16[1792,4096]{1,0:T(8,128)(2,1)} %bitcast.9, bf16[1792,256]{1,0:T(8,128)(2,1)} %bitcast.11, bf16[256,512]{1,0:T(8,128)(2,1)} %bitcast.13, bf16[64,4096]{1,0:T(8,128)(2,1)} %residual_in.1, ...), custom_call_target="tpu_custom_call" | custom-call | tf_op jit(solution)/shard_map/relay_boundary/pallas_call | solution.py:508
  110.8 0.0 copy-start
  110.8 0.8 copy-done
  111.6 0.0 copy-start.1
  111.6 0.8 copy-done.1
  112.4 36.9 %copy_out.1 = (bf16[64,4096]{1,0:T(8,128)(2,1)}, bf16[512,640]{1,0:T(8,128)(2,1)}) custom-call(bf16[64,4096]{1,0:T(8,128)(2,1)} %copy-done.1, bf16[512,640]{1,0:T(8,128)(2,1)} %copy-done), custom_call_target="tpu_custom_call" | custom-call | tf_op jit(solution)/shard_map/copy_out/pallas_call | solution.py:579
Async XLA Ops:
  110.8 0.8 copy-start
  111.6 0.8 copy-start.1

commit v4 on v2

--- a/solution.py
+++ b/solution.py
@@ -448,15 +448,23 @@
                 ag_copy(d, c, k, t).wait_send()
 
 
-def copy_out(stream_in, out_in, stream_ref, out_ref, sem):
-    copies = [
-        pltpu.make_async_copy(stream_in, stream_ref, sem.at[0]),
-        pltpu.make_async_copy(out_in, out_ref, sem.at[1]),
-    ]
-    for copy in copies:
-        copy.start()
-    for copy in copies:
-        copy.wait()
+def copy_out(stream_in, out_in, stream_ref, out_ref, stream, out, in_sem, out_sem):
+    reads, writes = [], []
+    for source, held, target, size in (
+        (out_in, out, out_ref, 64),
+        (stream_in, stream, stream_ref, CHUNK),
+    ):
+        for first in range(0, source.shape[0], size):
+            at, i = pl.ds(first, size), len(reads)
+            reads.append(pltpu.make_async_copy(source.at[at], held.at[at], in_sem.at[i]))
+            writes.append(pltpu.make_async_copy(held.at[at], target.at[at], out_sem.at[i]))
+    for read in reads:
+        read.start()
+    for read, write in zip(reads, writes):
+        read.wait()
+        write.start()
+    for write in writes:
+        write.wait()
 
 
 def per_device(
@@ -490,8 +498,8 @@
     outs = pl.pallas_call(
         functools.partial(kernel, T, S),
         out_shape=(
-            pltpu.VMEM((share, D), BF16),
-            pltpu.VMEM((rows, Q), BF16),
+            jax.ShapeDtypeStruct((share, D), BF16),
+            jax.ShapeDtypeStruct((rows, Q), BF16),
         ),
         in_specs=[any_spec] * 5 + [vmem] + [any_spec] * 3 + [vmem, smem, smem],
         out_specs=(vmem, vmem),
@@ -561,9 +569,15 @@
     return pl.pallas_call(
         copy_out,
         out_shape=tuple(jax.ShapeDtypeStruct(o.shape, o.dtype) for o in outs),
-        in_specs=[vmem] * 2,
+        in_specs=[any_spec] * 2,
         out_specs=(any_spec, any_spec),
-        scratch_shapes=[dma((2,))],
+        scratch_shapes=[
+            pltpu.VMEM((share, D), BF16),
+            pltpu.VMEM((rows, Q), BF16),
+            dma((rows // 64 + share // CHUNK,)),
+            dma((rows // 64 + share // CHUNK,)),
+        ],
+        compiler_params=pltpu.CompilerParams(vmem_limit_bytes=61 * 1024 * 1024),
         name="copy_out",
     )(*outs)
 

time: 113 us -> 112 us (level)
  local copies, waits for them, and re-layouts: 1.61 us -> 0 us
    unnamed x4 -> x0, local copies, waits for them, and re-layouts: 1.61 us -> none
where the time goes in v4:
time: 112 us
  Pallas kernels  111 us (99%)
    pallas_call x1, Pallas kernels, per_device(): pl.pallas_call(functools.partial(kernel, T, S), out_shape=(jax.ShapeDtype...  109 us

profile of v4, /device:TPU:0, one launch (start us, length us, event | category | flops | bytes accessed | tf_op | source)
XLA Modules:
  0.0 111.9 jit_solution(17196777396696690291)
XLA Ops:
  0.6 109.1 %relay_boundary.1 = (bf16[64,4096]{1,0:T(8,128)(2,1)}, bf16[512,640]{1,0:T(8,128)(2,1)}) custom-call(bf16[512,1792]{1,0:T(8,128)(2,1)} %hidden_in.1, bf16[1792,4096]{1,0:T(8,128)(2,1)} %bitcast.9, bf16[1792,256]{1,0:T(8,128)(2,1)} %bitcast.11, bf16[256,512]{1,0:T(8,128)(2,1)} %bitcast.13, bf16[64,4096]{1,0:T(8,128)(2,1)} %residual_in.1, ...), custom_call_target="tpu_custom_call" | custom-call | tf_op jit(solution)/shard_map/relay_boundary/pallas_call | solution.py:498
  109.7 2.2 %copy_out.1 = (bf16[64,4096]{1,0:T(8,128)(2,1)}, bf16[512,640]{1,0:T(8,128)(2,1)}) custom-call(bf16[64,4096]{1,0:T(8,128)(2,1)} %get-tuple-element.4.stream_in, bf16[512,640]{1,0:T(8,128)(2,1)} %get-tuple-element.5.out_in), custom_call_target="tpu_custom_call" | custom-call | tf_op jit(solution)/shard_map/copy_out/pallas_call | solution.py:569
